TPU v7x, 512 devices: a whole 4x8x8 slice. The times are simulated.
512 devices in a mesh: ep: 128 (over z, y, core), dec: 4 (over x).
Axes of the slice: x: 4, y: 8, z: 8, core: 2. Of those that a mesh axis runs over, the one named last changes fastest.
Arguments:
- tokens: bfloat16 [8192, 3584], P('ep', 'dec')
- expert_ids: int32 [8192, 8], P('ep'), may hold values from 0 to 127, all different within a row; in each aligned block of 64 rows (0 to 63, 64 to 127, ...) at most 5 rows name the same one
- route_scores: float32 [8192, 8], P('ep'), may hold values from -6 to 6
- up_weight: bfloat16 [128, 3584, 1024], P('ep', 'dec'), may hold values from -0.09375 to 0.09375
- down_weight: bfloat16 [128, 1024, 3584], P('ep', None, 'dec'), may hold values from -0.1875 to 0.1875
- latent_weight: bfloat16 [3584, 576], P('dec')
- latent_norm_gain: float32 [512], replicated, may hold values from 0.5 to 1.5
- page_owner: int32 [512], P('ep'), may hold values from 0 to 3, as said below
Outputs:
- combined: bfloat16 [8192, 3584], P('ep', 'dec')
- kv_pages: bfloat16 [8192, 576], P(('ep', 'dec'))
Inputs may be any that keep to these rules, and one draw needn't show every extreme that they name: `expert_ids`: each row names 8 different experts; among the 64 rows of one index of ep no expert is named by more than 5 rows, a bound that some block reaches. `page_owner`: within each aligned run of 4 pages every owner appears exactly 1 times.
All inputs are finite; a program needn't handle non-finite values.
Results may differ from a plain program's by a relative error of at most 0.02.
Values may be sent and summed in bfloat16 or wider, within the bound.
A program may use at most 64 MiB of HBM per device.

v0:
```python
import jax
import jax.numpy as jnp
from jax import lax
from jax.sharding import PartitionSpec as P

route_scale = 2.5


def finish_rows(latent_rows, positions, norm_gain):
    latent_rank_width = norm_gain.shape[0]
    compressed_latent = latent_rows[:, :latent_rank_width]
    inverse_rms = lax.rsqrt(
        jnp.mean(compressed_latent * compressed_latent, axis=1, keepdims=True) + 1e-06
    )
    normed = compressed_latent * inverse_rms * norm_gain[None, :]
    half_rotary_width = (latent_rows.shape[1] - latent_rank_width) // 2
    frequency = jnp.power(
        10000.0, -jnp.arange(half_rotary_width, dtype=jnp.float32) * 2.0 / (2 * half_rotary_width)
    )
    angles = positions[:, None] * frequency[None, :]
    cosine = jnp.cos(angles)
    sine_part = jnp.sin(angles)
    rotary_first_half = latent_rows[:, latent_rank_width : latent_rank_width + half_rotary_width]
    rotary_second_half = latent_rows[:, latent_rank_width + half_rotary_width :]
    rotated_first = rotary_first_half * cosine - rotary_second_half * sine_part
    rotated_second = rotary_second_half * cosine + rotary_first_half * sine_part
    return jnp.concatenate([normed, rotated_first, rotated_second], axis=1).astype(jnp.bfloat16)


def activate(partial_sums):
    summed = lax.psum(partial_sums.astype(jnp.bfloat16), "dec").astype(jnp.float32)
    return jax.nn.silu(summed).astype(jnp.bfloat16)


def expert_apply(row_block, up_matrix, down_matrix):
    partial_sums = jnp.dot(row_block, up_matrix, preferred_element_type=jnp.float32)
    hidden = activate(partial_sums)
    return jnp.dot(hidden, down_matrix, preferred_element_type=jnp.float32).astype(jnp.bfloat16)


def on_device(
    tokens,
    expert_ids,
    route_scores,
    up_weight,
    down_weight,
    latent_weight,
    latent_norm_gain,
    page_owner,
):
    tok_rows, quarter = tokens.shape
    top_count = expert_ids.shape[1]
    experts = lax.axis_size("ep")
    owners = lax.axis_size("dec")
    capacity = 5 * tok_rows * top_count // (4 * experts)
    ep_index = lax.axis_index("ep")
    dec_index = lax.axis_index("dec")
    latent_part = jnp.dot(tokens, latent_weight, preferred_element_type=jnp.float32)
    page_count = page_owner.shape[0]
    page_len = tok_rows // page_count
    per_owner = page_count // owners
    page_ids = jnp.arange(page_count, dtype=jnp.int32)
    same_owner = page_owner[:, None] == page_owner[None, :]
    earlier = page_ids[None, :] < page_ids[:, None]
    page_rank = jnp.sum(jnp.where(same_owner & earlier, 1, 0), axis=1)
    slot_of = page_owner * per_owner + page_rank
    page_at = jnp.sum(
        jnp.where(slot_of[None, :] == page_ids[:, None], page_ids[None, :], 0), axis=1
    )
    token_order = (
        page_at[:, None] * page_len + jnp.arange(page_len, dtype=jnp.int32)[None, :]
    ).reshape(-1)
    own_count = tok_rows // owners
    own_tokens = lax.dynamic_slice_in_dim(token_order, dec_index * own_count, own_count, 0)
    summed_latent = lax.psum(latent_part.astype(jnp.bfloat16), "dec").astype(jnp.float32)
    own_latent = jnp.take(summed_latent, own_tokens, axis=0)
    positions = (ep_index * tok_rows + own_tokens).astype(jnp.float32)
    kv_rows = finish_rows(own_latent, positions, latent_norm_gain)
    flat_ids = expert_ids.reshape(-1)
    expert_hits = (flat_ids[:, None] == jnp.arange(experts, dtype=jnp.int32)[None, :]).astype(
        jnp.int32
    )
    before = jnp.cumsum(expert_hits, axis=0) - expert_hits
    slot_rank = jnp.sum(before * expert_hits, axis=1)
    slot_dest = flat_ids * capacity + slot_rank
    outgoing = (
        jnp.zeros((experts * capacity, quarter), jnp.bfloat16)
        .at[slot_dest]
        .set(jnp.repeat(tokens, top_count, axis=0))
    )
    up_matrix = up_weight[0]
    down_matrix = down_weight[0]
    arrived_piece = lax.all_to_all(
        outgoing.reshape(experts, capacity, quarter), "ep", split_axis=0, concat_axis=0, tiled=True
    )
    sources = arrived_piece.shape[0]
    item_count = arrived_piece.shape[1]
    row_block = arrived_piece.reshape(sources * item_count, quarter)
    result = expert_apply(row_block, up_matrix, down_matrix).reshape(sources, item_count, quarter)
    returned = lax.all_to_all(result, "ep", split_axis=0, concat_axis=0, tiled=True).reshape(
        experts * capacity, quarter
    )
    gathered = jnp.take(returned, slot_dest, axis=0).reshape(tok_rows, top_count, quarter)
    gate_value = jax.nn.sigmoid(route_scores)
    route_weight = route_scale * gate_value / jnp.sum(gate_value, axis=1, keepdims=True)
    combined = jnp.sum(route_weight[:, :, None] * gathered.astype(jnp.float32), axis=1).astype(
        jnp.bfloat16
    )
    return (combined, kv_rows)


def solution(mesh):
    placed = (
        P("ep", "dec"),
        P("ep", None),
        P("ep", None),
        P("ep", "dec", None),
        P("ep", None, "dec"),
        P("dec", None),
        P(),
        P("ep"),
    )
    return jax.shard_map(
        on_device,
        mesh=mesh,
        in_specs=placed,
        out_specs=(P("ep", "dec"), P(("ep", "dec"), None)),
        check_vma=False,
    )
```

profile of v0, /device:TPU:8, one launch (start us, length us, event | category | flops | bytes accessed | tf_op | source)
XLA Modules:
  0.0 220.2 jit_solution(8393207264676322952)
XLA Ops:
  7.2 0.0 copy-start
  7.2 0.0 copy-start.2
  7.2 0.9 copy.25
  8.1 0.1 eq.50
  8.2 0.1 reshape.115
  8.3 0.7 broadcast_multiply_fusion
  9.0 0.1 copy.27
  9.1 0.2 fusion.22
  9.4 0.1 copy.31
  9.5 0.1 mul.107
  9.6 0.2 fusion.21
  9.8 0.0 copy-done.2
  9.9 2.8 %scatter_custom_fusion = bf16[640,896]{1,0:T(8,128)(2,1)S(1)} fusion(s32[512]{0:T(512)S(1)} %bitcast.39, bf16[]{:T(256)} %constant.37.clone.1, bf16[64,896]{1,0:T(8,128)(2,1)S(1)} %copy-done.2), kind=kCustom, calls=%fused_computation.19 | custom fusion | bytes 1261570 | tf_op jit(solution)/shard_map/scatter | solution.py:89
  12.7 1.5 reshape.118
  14.2 0.0 copy-start.1
  14.2 17.9 %all-to-all-start = ((bf16[128,5,896]{2,1,0:T(8,128)(2,1)}), bf16[128,5,896]{2,1,0:T(8,128)(2,1)}, u32[]{:S(2)}, u32[]{:S(2)}) async-start(bf16[128,5,896]{2,1,0:T(8,128)(2,1)} %reshape.118), calls=%async_computation | async-start | bytes 3670016 | tf_op jit(solution)/shard_map/all_to_all | solution.py:93
  32.1 0.0 all-reduce.3.cloned.1.call-start
  32.1 0.0 copy-done.1
  32.1 1.1 convolution_convert_fusion
  33.2 46.8 %all-to-all-done = bf16[128,5,896]{2,1,0:T(8,128)(2,1)} async-done(((bf16[128,5,896]{2,1,0:T(8,128)(2,1)}), bf16[128,5,896]{2,1,0:T(8,128)(2,1)}, u32[]{:S(2)}, u32[]{:S(2)}) %all-to-all-start) | async-done | bytes 1146912 | tf_op jit(solution)/shard_map/all_to_all | solution.py:93
  80.0 2.5 %reshape.119 = bf16[640,896]{1,0:T(8,128)(2,1)S(1)} reshape(bf16[128,5,896]{2,1,0:T(8,128)(2,1)} %all-to-all-done) | data formatting | bytes 2293760 | tf_op jit(solution)/shard_map/reshape | solution.py:98
  82.5 0.0 copy-done
  82.5 0.0 copy-start.7
  82.5 2.6 %fusion.8 = bf16[640,1024]{1,0:T(8,128)(2,1)} fusion(bf16[640,896]{1,0:T(8,128)(2,1)S(1)} %reshape.119, bf16[1,896,1024]{2,1,0:T(8,128)(2,1)S(1)} %copy-done), kind=kOutput, calls=%fused_computation.14 | convolution fusion | flops 1175060480 | bytes 4292608 | tf_op jit(solution)/shard_map/dot_general | solution.py:36
  85.1 0.0 all-reduce.3.cloned.1.call-update
  85.2 0.0 copy-done.7
  85.2 0.2 select_reduce_fusion.1
  85.4 0.1 select_reduce_fusion
  85.5 52.6 %all-reduce.3.cloned.1.call-done = (bf16[640,1024]{1,0:T(8,128)(2,1)}, bf16[64,576]{1,0:T(8,128)(2,1)}) async-done(((bf16[640,1024]{1,0:T(8,128)(2,1)}, bf16[64,576]{1,0:T(8,128)(2,1)}), (bf16[640,1024]{1,0:T(8,128)(2,1)}, bf16[64,576]{1,0:T(8,128)(2,1)})) %all-reduce.3.cloned.1.call-update) | async-done | bytes 1384464 | tf_op jit(solution)/shard_map/psum | solution.py:31
  138.0 3.4 %fusion.11 = bf16[640,896]{1,0:T(8,128)(2,1)S(1)} fusion(bf16[1,1024,896]{2,1,0:T(8,128)(2,1)} %param.12, bf16[640,1024]{1,0:T(8,128)(2,1)} %get-tuple-element.2), kind=kOutput, calls=%fused_computation.15 | convolution fusion | flops 1178910720 | bytes 4292608 | tf_op jit(solution)/shard_map/dot_general | solution.py:38
  141.5 1.5 reshape.120
  143.0 0.0 copy-start.4
  143.0 0.0 copy-start.5
  143.0 0.0 copy-start.3
  143.0 0.0 copy-start.6
  143.0 14.7 %all-to-all-start.1 = ((bf16[128,5,896]{2,1,0:T(8,128)(2,1)}), bf16[128,5,896]{2,1,0:T(8,128)(2,1)}, u32[]{:S(2)}, u32[]{:S(2)}) async-start(bf16[128,5,896]{2,1,0:T(8,128)(2,1)} %reshape.120), calls=%async_computation.1 | async-start | bytes 3670016 | tf_op jit(solution)/shard_map/all_to_all | solution.py:100
  157.7 0.1 iota_add_fusion
  157.8 0.1 reduce_sum.60
  157.9 0.1 add.106
  157.9 0.1 copy.29
  158.0 0.0 copy-done.4
  158.0 0.1 copy.30
  158.1 0.0 copy-done.5
  158.2 0.1 copy.24
  158.3 0.1 add_convert_fusion
  158.4 0.1 compare_and_fusion.1
  158.5 0.0 copy-done.3
  158.5 0.6 gather_fusion.1
  159.1 0.1 broadcast_select_fusion
  159.2 0.1 multiply_reduce_fusion.1
  159.3 0.1 fusion.30
  159.4 0.0 copy-done.6
  159.4 0.1 multiply_convert_fusion
  159.5 0.7 pad_maximum_fusion
  160.2 45.5 %all-to-all-done.1 = bf16[128,5,896]{2,1,0:T(8,128)(2,1)} async-done(((bf16[128,5,896]{2,1,0:T(8,128)(2,1)}), bf16[128,5,896]{2,1,0:T(8,128)(2,1)}, u32[]{:S(2)}, u32[]{:S(2)}) %all-to-all-start.1) | async-done | bytes 1146912 | tf_op jit(solution)/shard_map/all_to_all | solution.py:100
  205.6 2.5 %reshape.121 = bf16[640,896]{1,0:T(8,128)(2,1)S(1)} reshape(bf16[128,5,896]{2,1,0:T(8,128)(2,1)} %all-to-all-done.1) | data formatting | bytes 2293760 | tf_op jit(solution)/shard_map/reshape | solution.py:100
  208.1 2.8 %gather_fusion = bf16[512,896]{1,0:T(8,128)(2,1)} fusion(bf16[640,896]{1,0:T(8,128)(2,1)S(1)} %reshape.121, s32[1024]{0:T(1024)S(1)} %pad_clamp_fusion.1), kind=kCustom, calls=%fused_computation | custom fusion | bytes 1837056 | tf_op jit(solution)/shard_map/jit(_take)/gather | solution.py:103
  210.9 2.5 %multiply_reduce_fusion = bf16[64,896]{1,0:T(8,128)(2,1)} fusion(bf16[512,896]{1,0:T(8,128)(2,1)} %gather_fusion, f32[64,8]{1,0:T(8,128)S(1)} %copy.24, pred[64,8]{1,0:T(8,128)(4,1)S(1)} %copy.30), kind=kLoop, calls=%fused_computation.13 | loop fusion | flops 1777664 | bytes 1034752 | tf_op jit(solution)/shard_map/reduce_sum | solution.py:106
  (17 shorter events, 0.2 us)
Async XLA Ops:
  7.2 75.3 %copy-start = (bf16[1,896,1024]{2,1,0:T(8,128)(2,1)S(1)}, bf16[1,896,1024]{2,1,0:T(8,128)(2,1)}, u32[]{:S(2)}) copy-start(bf16[1,896,1024]{2,1,0:T(8,128)(2,1)} %param.11) | copy-start | bytes 5505028
  7.2 2.7 %copy-start.2 = (bf16[64,896]{1,0:T(8,128)(2,1)S(1)}, bf16[64,896]{1,0:T(8,128)(2,1)}, u32[]{:S(2)}) copy-start(bf16[64,896]{1,0:T(8,128)(2,1)} %param.8) | copy-start | bytes 344068
  14.2 18.0 %copy-start.1 = (bf16[896,576]{0,1:T(8,128)(2,1)S(1)}, bf16[896,576]{0,1:T(8,128)(2,1)}, u32[]{:S(2)}) copy-start(bf16[896,576]{0,1:T(8,128)(2,1)} %param.13) | copy-start | bytes 3096580
  14.2 65.9 %all-to-all-start = ((bf16[128,5,896]{2,1,0:T(8,128)(2,1)}), bf16[128,5,896]{2,1,0:T(8,128)(2,1)}, u32[]{:S(2)}, u32[]{:S(2)}) async-start(bf16[128,5,896]{2,1,0:T(8,128)(2,1)} %reshape.118), calls=%async_computation | async-start | bytes 3670016 | tf_op jit(solution)/shard_map/all_to_all | solution.py:93
  32.1 106.0 %all-reduce.3.cloned.1.call-start = ((), (), s32[]{:S(2)}) async-start(), calls=%async_computation.2 | async-start | bytes 2785280 | tf_op jit(solution)/shard_map/psum | solution.py:31
  82.5 2.7 %copy-start.7 = (s32[4]{0:T(128)S(1)}, s32[4]{0:T(128)}, u32[]{:S(2)}) copy-start(s32[4]{0:T(128)} %param.15) | copy-start | bytes 52
  143.0 15.0 %copy-start.4 = (s32[64,8]{0,1:T(8,128)S(1)}, s32[64,8]{0,1:T(8,128)}, u32[]{:S(2)}) copy-start(s32[64,8]{0,1:T(8,128)} %param.9) | copy-start | bytes 6148
  143.0 15.2 %copy-start.5 = (f32[64,8]{0,1:T(8,128)S(1)}, f32[64,8]{0,1:T(8,128)}, u32[]{:S(2)}) copy-start(f32[64,8]{0,1:T(8,128)} %param.10) | copy-start | bytes 6148
  143.0 15.5 %copy-start.3 = (bf16[64,576]{1,0:T(8,128)(2,1)S(1)}, bf16[64,576]{1,0:T(8,128)(2,1)}, u32[]{:S(2)}) copy-start(bf16[64,576]{1,0:T(8,128)(2,1)} %get-tuple-element.3) | copy-start | bytes 221188
  143.0 16.5 %copy-start.6 = (f32[512]{0:T(512)S(1)}, f32[512]{0:T(512)}, u32[]{:S(2)}) copy-start(f32[512]{0:T(512)} %param.14) | copy-start | bytes 6148
  143.0 62.7 %all-to-all-start.1 = ((bf16[128,5,896]{2,1,0:T(8,128)(2,1)}), bf16[128,5,896]{2,1,0:T(8,128)(2,1)}, u32[]{:S(2)}, u32[]{:S(2)}) async-start(bf16[128,5,896]{2,1,0:T(8,128)(2,1)} %reshape.120), calls=%async_computation.1 | async-start | bytes 3670016 | tf_op jit(solution)/shard_map/all_to_all | solution.py:100
Sparse Core Ops, SparseCore 0:
  85.3 52.7 all-reduce.2
where the time goes:
time: 221 us; the launch traced here: 220 us
  waiting for transfers between devices  145 us (66%)
  starting transfers between devices  32.6 us (15%)
  local copies, waits for them, and re-layouts  15.9 us (7%)
  between operations  14.3 us (6%)
  matrix products  7.15 us (3%)
  other arithmetic  5.46 us (2%)
    psum x1, waiting for transfers between devices, activate(): lax.psum(partial_sums.astype(jnp.bfloat16), 'dec').astype(jnp.float32)  52.6 us
    all_to_all x1, waiting for transfers between devices, on_device(): lax.all_to_all(outgoing.reshape(experts, capacity, quarter), 'ep', split_...  46.8 us
    all_to_all x1, waiting for transfers between devices, on_device(): lax.all_to_all(result, 'ep', split_axis=0, concat_axis=0, tiled=True)  45.5 us
    all_to_all x1, starting transfers between devices, on_device(): lax.all_to_all(outgoing.reshape(experts, capacity, quarter), 'ep', split_...  17.9 us
    all_to_all x1, starting transfers between devices, on_device(): lax.all_to_all(result, 'ep', split_axis=0, concat_axis=0, tiled=True)  14.7 us
  transfers between devices with their start and end apart: 3, of which 3 were waited for; matrix products, arithmetic and copies ran while one was open for 2% of the time, Pallas kernels for 0%

commit v1 on v0

v1 whole, which is shorter than its diff:
```python
import functools

import jax
import jax.numpy as jnp
import numpy as np
from jax import lax
from jax.experimental import pallas as pl
from jax.experimental.pallas import tpu as pltpu
from jax.sharding import PartitionSpec as P

MESH = pl.DeviceIdType.MESH
bf16 = jnp.bfloat16
f32 = jnp.float32

ROUTE_SCALE = 2.5
N = 8
TOK = 64
TOP = 8
CAP = 5
MSG = N * CAP
QUARTER = 896
HID = 1024
LATENT = 512
KV = 576
PAGE = 16
PACK = 2304
CHUNKS = ((0, 1), (7, 2), (6, 3), (5, 4))
ROWS = 4 * MSG


def dot(a, b):
    return jnp.dot(a, b, preferred_element_type=f32)


def pack(ref, at, rows):
    ref[at, :, 0:QUARTER] = rows[0:16].astype(bf16)
    ref[at, :, QUARTER : 2 * QUARTER] = rows[16:32].astype(bf16)
    tail = rows[32:40]
    rest = jnp.concatenate([tail[:, 512:QUARTER], jnp.zeros((8, 128), f32)], axis=1)
    ref[at, :, 2 * QUARTER : PACK] = jnp.concatenate([tail[:, 0:512], rest], axis=0).astype(bf16)


def pack_pair(ref, first, second, rows):
    pack(ref, first, jnp.concatenate([rows[0:32], rows[64:72]], axis=0))
    pack(ref, second, jnp.concatenate([rows[32:64], rows[72:80]], axis=0))


def unpack_pair(ref, first, second):
    heads, tails = [], []
    for at in (first, second):
        heads += [ref[at, :, 0:QUARTER], ref[at, :, QUARTER : 2 * QUARTER]]
        tail = ref[at, :, 2 * QUARTER : PACK].astype(f32)
        tails.append(jnp.concatenate([tail[0:8], tail[8:16, 0 : QUARTER - 512]], axis=1))
    tail = jnp.concatenate(tails, axis=0).astype(bf16)
    return jnp.concatenate(heads + [tail], axis=0)


def kernel(
    tok_ref,
    ids_ref,
    scores_ref,
    up_hbm,
    down_hbm,
    lat_hbm,
    gain_ref,
    owner_ref,
    freq_ref,
    out_ref,
    kv_ref,
    up_ref,
    down_ref,
    lat_ref,
    line_tok,
    line_meta,
    code_ref,
    wsel_ref,
    disp_out,
    disp_in,
    back_out,
    back_in,
    chain_out,
    chain_in,
    part_ref,
    full_out,
    full_in,
    hid_ref,
    pick_ref,
    sum_ref,
    line_out,
    line_in,
    lat_out,
    lat_own,
    lat_in,
    load_sem,
    tok_send,
    tok_recv,
    meta_send,
    meta_recv,
    disp_send,
    disp_recv,
    back_send,
    back_recv,
    chain_send,
    chain_recv,
    full_send,
    full_recv,
    hid_send,
    hid_recv,
    line_send,
    line_recv,
    lat_send,
    lat_recv,
):
    ep = lax.axis_index("ep")
    x = lax.axis_index("dec")
    core = lax.rem(ep, 2)
    chip = lax.div(ep, 2)
    z = lax.div(chip, N)
    y = lax.rem(chip, N)
    on_z = core == 0
    mine = jnp.where(on_z, z, y)
    cross = jnp.where(on_z, y, z)

    def wrap(v):
        return lax.rem(v + 2 * N, N)

    def line_dev(step):
        place = wrap(mine + step)
        zz = jnp.where(on_z, place, z)
        yy = jnp.where(on_z, y, place)
        return ((zz * N + yy) * 2 + core, x)

    def expert_dev(step, c):
        place = wrap(cross + step)
        zz = jnp.where(on_z, z, place)
        yy = jnp.where(on_z, place, y)
        return ((zz * N + yy) * 2 + c, x)

    def source_dev(c_src, step):
        if c_src == 0:
            return ((z * N + wrap(y - step)) * 2, x)
        return ((wrap(z - step) * N + y) * 2 + 1, x)

    def dec_dev(step):
        return (ep, lax.rem(x + step + 4, 4))

    sent = []

    def send(src, dst, s_sem, r_sem, dev):
        copy = pltpu.make_async_remote_copy(
            src_ref=src, dst_ref=dst, send_sem=s_sem, recv_sem=r_sem, device_id=dev, device_id_type=MESH
        )
        copy.start()
        sent.append(copy)

    def arrived(dst, sem):
        pltpu.make_async_copy(dst, dst, sem).wait()

    loads = [
        pltpu.make_async_copy(lat_hbm, lat_ref, load_sem.at[0]),
        pltpu.make_async_copy(up_hbm.at[0], up_ref, load_sem.at[1]),
        pltpu.make_async_copy(down_hbm.at[0], down_ref, load_sem.at[2]),
    ]
    for load in loads:
        load.start()

    barrier = pltpu.get_barrier_semaphore()

    def greet(dev):
        pl.semaphore_signal(barrier, inc=1, device_id=dev, device_id_type=MESH)

    greet(((z * N + y) * 2 + 1 - core, x))
    for step in range(1, N):
        for c in range(2):
            greet(((z * N + wrap(y + step)) * 2 + c, x))
            greet(((wrap(z + step) * N + y) * 2 + c, x))
    for step in range(1, 4):
        greet(dec_dev(step))

    gate = jax.nn.sigmoid(scores_ref[...])
    weight = ROUTE_SCALE * gate / jnp.sum(gate, axis=1, keepdims=True)
    line_meta[0] = jnp.concatenate([ids_ref[...].astype(f32).T, weight.T], axis=1)
    line_tok[0] = tok_ref[...]

    lane = lax.broadcasted_iota(jnp.int32, (TOK, TOK), 1)
    row = lax.broadcasted_iota(jnp.int32, (TOK, TOK), 0)
    owner_of = jnp.zeros((TOK, TOK), jnp.int32)
    page = jnp.int32(0)
    for p in range(4):
        owner_of = jnp.where((lane >> 4) == p, owner_ref[p], owner_of)
        page = page + jnp.where(owner_ref[p] == x, p, 0)
    wanted = lax.rem((row >> 4) + x, 4)
    order = jnp.where((owner_of == wanted) & ((lane & 15) == (row & 15)), 1.0, 0.0).astype(bf16)
    ordered = dot(order, tok_ref[...]).astype(bf16)
    loads[0].wait()
    latent = dot(ordered, lat_ref[...])
    lat_own[...] = latent[0:PAGE]
    lat_out[...] = latent[PAGE:].astype(bf16).reshape(3, PAGE, KV)

    pl.semaphore_wait(barrier, 4 * (N - 1) + 4)

    def pass_on(k, h, plus):
        at = (2 * (k - 1) + h) if k < 4 else 6
        at = at if plus else 7 + at
        rows = pl.ds(h * 32, 32)
        slot = k if plus else N - k
        prev = k - 1 if plus else (N - k + 1) % N
        src = tok_ref.at[rows] if k == 1 else line_tok.at[prev, rows]
        send(src, line_tok.at[slot, rows], tok_send.at[at], tok_recv.at[at], line_dev(1 if plus else -1))

    def taken(k, h, plus):
        at = (2 * (k - 1) + h) if k < 4 else 6
        at = at if plus else 7 + at
        arrived(line_tok.at[k if plus else N - k, pl.ds(h * 32, 32)], tok_recv.at[at])

    for h in range(2):
        for plus in (True, False):
            pass_on(1, h, plus)
    for step in range(1, N):
        send(line_meta.at[0], line_meta.at[step], meta_send.at[step - 1], meta_recv.at[step - 1], line_dev(step))
    for step in range(1, 4):
        send(lat_out.at[step - 1], lat_in.at[step - 1], lat_send.at[step - 1], lat_recv.at[step - 1], dec_dev(step))
    for k in range(1, 4):
        for h in range(2):
            for plus in (True, False):
                taken(k, h, plus)
                if k < 3 or h == (0 if plus else 1):
                    pass_on(k + 1, h, plus)

    for step in range(1, N):
        arrived(line_meta.at[step], meta_recv.at[step - 1])
    low = lax.broadcasted_iota(jnp.int32, (TOP, 128), 1) < TOK
    ids, weights = [], []
    for pair in range(4):
        even, odd = line_meta[2 * pair], line_meta[2 * pair + 1]
        ids.append(jnp.where(low, even, pltpu.roll(odd, TOK, 1)))
        weights.append(jnp.where(low, pltpu.roll(even, TOK, 1), odd))
    ids = jnp.concatenate(ids, axis=1)
    weights = jnp.concatenate(weights, axis=1)
    number = lax.broadcasted_iota(jnp.int32, (16, 512), 0)
    place = lax.rem(cross + (number >> 1), N)
    expert = jnp.where(on_z, 16 * mine + 2 * place, 16 * place + 2 * mine) + (number & 1)
    expert = expert.astype(f32)
    hits = jnp.zeros((16, 512), f32)
    wsel = jnp.zeros((16, 512), f32)
    for k in range(TOP):
        match = ids[k : k + 1, :] == expert
        hits = jnp.where(match, 1.0, hits)
        wsel = jnp.where(match, weights[k : k + 1, :], wsel)
    before_r = lax.broadcasted_iota(jnp.int32, (128, 128), 0)
    before_c = lax.broadcasted_iota(jnp.int32, (128, 128), 1)
    before = jnp.where((before_r < before_c) & ((before_r >> 6) == (before_c >> 6)), 1.0, 0.0).astype(bf16)
    rank = jnp.concatenate(
        [dot(hits[:, 128 * i : 128 * i + 128].astype(bf16), before) for i in range(4)], axis=1
    )
    code_ref[...] = jnp.where(hits > 0.5, rank, -1.0)
    wsel_ref[...] = wsel

    slot_row = lax.broadcasted_iota(jnp.int32, (MSG, 512), 0)
    slot_lane = lax.broadcasted_iota(jnp.int32, (MSG, 512), 1)
    pattern = jnp.where((slot_lane >> 6) == (slot_row & 7), slot_row >> 3, -2).astype(f32)

    def picks(step, weighted):
        parts = []
        for c in range(2):
            at = 2 * step + c
            value = wsel_ref[at : at + 1, :] if weighted else 1.0
            parts.append(jnp.where(code_ref[at : at + 1, :] == pattern, value, 0.0))
        a, b = parts
        return jnp.concatenate([a[0:32], b[0:32], a[32:40], b[32:40]], axis=0)

    for h, plus in ((0, True), (1, False)):
        taken(4, h, plus)

    local = []
    for step in [s for chunk in CHUNKS for s in chunk]:
        rows = dot(picks(step, False).astype(bf16), line_tok[...].reshape(N * TOK, QUARTER))
        pack_pair(disp_out, 2 * step, 2 * step + 1, rows)
        slot = N * core + step
        if step == 0:
            copy = pltpu.make_async_copy(disp_out.at[core], disp_in.at[slot], disp_recv.at[slot])
            copy.start()
            other = 1 - core
            send(disp_out.at[other], disp_in.at[slot], disp_send.at[other], disp_recv.at[slot], expert_dev(0, other))
        else:
            for c in range(2):
                at = 2 * step + c
                send(disp_out.at[at], disp_in.at[slot], disp_send.at[at], disp_recv.at[slot], expert_dev(step, c))

    for j, chunk in enumerate(CHUNKS):
        both = jnp.concatenate([picks(step, True) for step in chunk], axis=0)
        pick_ref[j] = both.T.astype(bf16)

    for step in range(1, 4):
        arrived(lat_in.at[step - 1], lat_recv.at[step - 1])
    total = lat_own[...]
    for step in range(3):
        total = total + lat_in[step].astype(f32)
    comp = total[:, 0:LATENT]
    scale = lax.rsqrt(jnp.sum(comp * comp, axis=1, keepdims=True) * (1.0 / LATENT) + 1e-6)
    kv_ref[:, 0:LATENT] = (comp * scale * gain_ref[...]).astype(bf16)
    half = (KV - LATENT) // 2
    first, second = total[:, LATENT : LATENT + half], total[:, LATENT + half :]
    token = (ep * TOK + page * PAGE + lax.broadcasted_iota(jnp.int32, (PAGE, half), 0)).astype(f32)
    angle = token * freq_ref[...]
    cos, sin = jnp.cos(angle), jnp.sin(angle)
    kv_ref[:, LATENT:] = jnp.concatenate(
        [first * cos - second * sin, second * cos + first * sin], axis=1
    ).astype(bf16)

    loads[1].wait()
    loads[2].wait()

    def quarter_of(step):
        return pl.ds(pl.multiple_of(lax.rem(x + step + 4, 4) * 256, 256), 256)

    def stage_up(j):
        for step in CHUNKS[j]:
            for c in range(2):
                arrived(disp_in.at[N * c + step], disp_recv.at[N * c + step])
        block = jnp.concatenate([unpack_pair(disp_in, step, N + step) for step in CHUNKS[j]], axis=0)
        part = dot(block, up_ref[:, quarter_of(2)])
        for d in range(2):
            chain_out[j, d] = part[:, 128 * d : 128 * d + 128].astype(bf16)
            at = 2 * j + d
            send(
                chain_out.at[j, d],
                chain_in.at[j, d],
                chain_send.at[at],
                chain_recv.at[at],
                dec_dev(1 if d == 0 else -1),
            )
        part_ref[j, 0] = dot(block, up_ref[:, quarter_of(1)])
        part_ref[j, 1] = dot(block, up_ref[:, quarter_of(-1)])
        part_ref[j, 2] = dot(block, up_ref[:, quarter_of(0)])

    def stage_chain(j):
        for d in range(2):
            at = 2 * j + d
            arrived(chain_in.at[j, d], chain_recv.at[at])
            for half in range(2):
                value = part_ref[j, d, :, 128 * half : 128 * half + 128]
                if half == d:
                    value = value + chain_in[j, d].astype(f32)
                full_out[j, d, half] = value.astype(bf16)
            send(
                full_out.at[j, d],
                full_in.at[j, d],
                full_send.at[at],
                full_recv.at[at],
                dec_dev(1 if d == 0 else -1),
            )

    def stage_hidden(j):
        for d in range(2):
            arrived(full_in.at[j, d], full_recv.at[2 * j + d])
        for half in range(2):
            pre = part_ref[j, 2, :, 128 * half : 128 * half + 128]
            pre = pre + full_in[j, 0, half].astype(f32) + full_in[j, 1, half].astype(f32)
            hid_ref[j, 0, half] = (pre / (1.0 + jnp.exp(-pre))).astype(bf16)
        for d in range(2):
            send(
                hid_ref.at[j, 0],
                hid_ref.at[j, 1 + d],
                hid_send.at[4 * j + d],
                hid_recv.at[4 * j + d],
                dec_dev(1 if d == 0 else -1),
            )

    def stage_pass(j):
        for d in range(2):
            arrived(hid_ref.at[j, 1 + d], hid_recv.at[4 * j + d])
            send(
                hid_ref.at[j, 1 + d, d],
                hid_ref.at[j, 3, d],
                hid_send.at[4 * j + 2 + d],
                hid_recv.at[4 * j + 2 + d],
                dec_dev(1 if d == 0 else -1),
            )

    def stage_down(j):
        total = None
        for place, step in ((0, 0), (1, -1), (2, 1), (3, 2)):
            if place == 3:
                for d in range(2):
                    arrived(hid_ref.at[j, 3, d], hid_recv.at[4 * j + 2 + d])
            hidden = jnp.concatenate([hid_ref[j, place, 0], hid_ref[j, place, 1]], axis=1)
            term = dot(hidden, down_ref[quarter_of(step), :])
            total = term if total is None else total + term
        for i, step in enumerate(CHUNKS[j]):
            pack_pair(back_out, step, N + step, total[2 * MSG * i : 2 * MSG * (i + 1)])
            slot = 2 * step + core
            for c in range(2):
                at = N * c + step
                if step:
                    send(back_out.at[at], back_in.at[slot], back_send.at[at], back_recv.at[slot], source_dev(c, step))
            if step == 0:
                own, other = N * core, N * (1 - core)
                pltpu.make_async_copy(back_out.at[own], back_in.at[core], back_recv.at[core]).start()
                send(
                    back_out.at[other],
                    back_in.at[core],
                    back_send.at[other],
                    back_recv.at[core],
                    ((z * N + y) * 2 + 1 - core, x),
                )

    def stage_sum(j):
        for step in CHUNKS[j]:
            for c in range(2):
                arrived(back_in.at[2 * step + c], back_recv.at[2 * step + c])
        block = jnp.concatenate([unpack_pair(back_in, 2 * step, 2 * step + 1) for step in CHUNKS[j]], axis=0)
        term = dot(pick_ref[j], block)
        if j == 0:
            sum_ref[...] = term
        else:
            sum_ref[...] = sum_ref[...] + term

    stage_up(0)
    stage_chain(0)
    stage_up(1)
    stage_hidden(0)
    stage_chain(1)
    stage_pass(0)
    stage_up(2)
    stage_hidden(1)
    stage_chain(2)
    stage_down(0)
    stage_pass(1)
    stage_up(3)
    stage_hidden(2)
    stage_chain(3)
    stage_down(1)
    stage_pass(2)
    stage_hidden(3)
    stage_sum(0)
    stage_down(2)
    stage_pass(3)
    stage_sum(1)
    stage_down(3)
    stage_sum(2)
    stage_sum(3)

    for step in range(1, N):
        line_out[step - 1] = sum_ref[step * TOK : (step + 1) * TOK].astype(bf16)
        send(line_out.at[step - 1], line_in.at[step - 1], line_send.at[step - 1], line_recv.at[step - 1], line_dev(-step))
    total = sum_ref[0:TOK]
    for step in range(1, N):
        arrived(line_in.at[step - 1], line_recv.at[step - 1])
        total = total + line_in[step - 1].astype(f32)
    out_ref[...] = total.astype(bf16)

    for copy in sent:
        copy.wait_send()


def on_device(tokens, expert_ids, route_scores, up_weight, down_weight, latent_weight, latent_norm_gain, page_owner):
    half = (KV - LATENT) // 2
    freq = np.power(10000.0, -np.arange(half, dtype=np.float64) / half).astype(np.float32)
    vmem = pl.BlockSpec(memory_space=pltpu.VMEM)
    hbm = pl.BlockSpec(memory_space=pl.ANY)
    smem = pl.BlockSpec(memory_space=pltpu.SMEM)
    dma = pltpu.SemaphoreType.DMA
    return pl.pallas_call(
        kernel,
        out_shape=(
            jax.ShapeDtypeStruct((TOK, QUARTER), bf16),
            jax.ShapeDtypeStruct((PAGE, KV), bf16),
        ),
        in_specs=[vmem, vmem, vmem, hbm, hbm, hbm, vmem, smem, vmem],
        out_specs=(vmem, vmem),
        scratch_shapes=[
            pltpu.VMEM((QUARTER, HID), bf16),
            pltpu.VMEM((HID, QUARTER), bf16),
            pltpu.VMEM((QUARTER, KV), bf16),
            pltpu.VMEM((N, TOK, QUARTER), bf16),
            pltpu.VMEM((N, TOP, 128), f32),
            pltpu.VMEM((16, 512), f32),
            pltpu.VMEM((16, 512), f32),
            pltpu.VMEM((16, 16, PACK), bf16),
            pltpu.VMEM((16, 16, PACK), bf16),
            pltpu.VMEM((16, 16, PACK), bf16),
            pltpu.VMEM((16, 16, PACK), bf16),
            pltpu.VMEM((4, 2, ROWS, 128), bf16),
            pltpu.VMEM((4, 2, ROWS, 128), bf16),
            pltpu.VMEM((4, 3, ROWS, 256), f32),
            pltpu.VMEM((4, 2, 2, ROWS, 128), bf16),
            pltpu.VMEM((4, 2, 2, ROWS, 128), bf16),
            pltpu.VMEM((4, 4, 2, ROWS, 128), bf16),
            pltpu.VMEM((4, N * TOK, ROWS), bf16),
            pltpu.VMEM((N * TOK, QUARTER), f32),
            pltpu.VMEM((7, TOK, QUARTER), bf16),
            pltpu.VMEM((7, TOK, QUARTER), bf16),
            pltpu.VMEM((3, PAGE, KV), bf16),
            pltpu.VMEM((PAGE, KV), f32),
            pltpu.VMEM((3, PAGE, KV), bf16),
            dma((3,)),
            dma((14,)),
            dma((14,)),
            dma((7,)),
            dma((7,)),
            dma((16,)),
            dma((16,)),
            dma((16,)),
            dma((16,)),
            dma((8,)),
            dma((8,)),
            dma((8,)),
            dma((8,)),
            dma((16,)),
            dma((16,)),
            dma((7,)),
            dma((7,)),
            dma((3,)),
            dma((3,)),
        ],
        compiler_params=pltpu.CompilerParams(
            collective_id=0, has_side_effects=True, vmem_limit_bytes=40 * 1024 * 1024
        ),
    )(
        tokens,
        expert_ids,
        route_scores,
        up_weight,
        down_weight,
        latent_weight,
        latent_norm_gain.reshape(1, LATENT),
        page_owner,
        jnp.asarray(freq).reshape(1, half),
    )


def solution(mesh):
    placed = (
        P("ep", "dec"),
        P("ep", None),
        P("ep", None),
        P("ep", "dec", None),
        P("ep", None, "dec"),
        P("dec", None),
        P(),
        P("ep"),
    )
    return jax.shard_map(
        on_device,
        mesh=mesh,
        in_specs=placed,
        out_specs=(P("ep", "dec"), P(("ep", "dec"), None)),
        check_vma=False,
    )
```

time: 221 us -> 102 us (0.46)
  the two profiles are of different devices: /device:TPU:8 before, /device:TPU:22 now
where the time goes in v1:
time: 102 us
  Pallas kernels  94.3 us (92%)
  local copies, waits for them, and re-layouts  6.48 us (6%)
    pallas_call x1, Pallas kernels, on_device(): pl.pallas_call(kernel, out_shape=(jax.ShapeDtypeStruct((TOK, QUARTER), bf...  94.3 us
    unnamed x17, local copies, waits for them, and re-layouts  6.48 us

profile of v1, /device:TPU:22, one launch (start us, length us, event | category | flops | bytes accessed | tf_op | source)
XLA Modules:
  0.0 101.5 jit_solution(15555164726531504812)
XLA Ops:
  0.6 0.0 copy-start.5
  0.6 0.0 copy-start.4
  0.7 0.0 copy-start.3
  0.7 0.0 copy-start
  0.7 0.0 copy-start.2
  0.7 0.9 copy.11.ids_ref
  1.6 0.8 copy.12.scores_ref
  2.4 2.0 %copy.13.lat_hbm = bf16[896,576]{1,0:T(8,128)(2,1)S(1)} copy(bf16[896,576]{0,1:T(8,128)(2,1)} %param.14) | data formatting | bytes 2064384 | tf_op args[5]
  4.4 0.0 copy-done.5
  4.4 0.0 copy-done.4
  4.4 0.0 copy-done.3
  4.4 0.0 copy-done
  4.4 0.0 copy-done.2
  4.4 0.0 copy-start.1
  4.5 1.5 %copy-done.1 = bf16[1,1024,896]{2,1,0:T(8,128)(2,1)S(1)} copy-done((bf16[1,1024,896]{2,1,0:T(8,128)(2,1)S(1)}, bf16[1,1024,896]{2,1,0:T(8,128)(2,1)}, u32[]{:S(2)}) %copy-start.1) | copy-done | bytes 1835032
  6.0 94.3 %shard_map.104 = (bf16[64,896]{1,0:T(8,128)(2,1)S(1)}, bf16[16,576]{1,0:T(8,128)(2,1)S(1)}) custom-call(bf16[64,896]{1,0:T(8,128)(2,1)S(1)} %copy-done.2, s32[64,8]{1,0:T(8,128)S(1)} %copy.11.ids_ref, f32[64,8]{1,0:T(8,128)S(1)} %copy.12.scores_ref, bf16[1,896,1024]{2,1,0:T(8,128)(2,1)S(1)} %copy-done, bf16[1,1024,896]{2,1,0:T(8,128)(2,1)S(1)} %copy-done.1, ...), custom_call_target="tpu_custom_call" | custom-call | tf_op jit(solution)/shard_map/pallas_call | solution.py:464
  100.3 0.6 copy.16
  100.9 0.6 copy.17
Async XLA Ops:
  0.6 3.8 %copy-start.5 = (f32[1,32]{1,0:T(1,128)S(1)}, f32[1,32]{1,0:T(1,128)}, u32[]{:S(2)}) copy-start(f32[1,32]{1,0:T(1,128)} %constant.9.freq_ref) | copy-start | bytes 388
  0.6 3.8 %copy-start.4 = (s32[4]{0:T(128)S(1)}, s32[4]{0:T(128)}, u32[]{:S(2)}) copy-start(s32[4]{0:T(128)} %owner_ref.1) | copy-start | bytes 52
  0.7 3.8 %copy-start.3 = (f32[512]{0:T(512)S(1)}, f32[512]{0:T(512)}, u32[]{:S(2)}) copy-start(f32[512]{0:T(512)} %param.15) | copy-start | bytes 6148
  0.7 3.8 %copy-start = (bf16[1,896,1024]{2,1,0:T(8,128)(2,1)S(1)}, bf16[1,896,1024]{2,1,0:T(8,128)(2,1)}, u32[]{:S(2)}) copy-start(bf16[1,896,1024]{2,1,0:T(8,128)(2,1)} %up_hbm.1) | copy-start | bytes 5505028
  0.7 3.8 %copy-start.2 = (bf16[64,896]{1,0:T(8,128)(2,1)S(1)}, bf16[64,896]{1,0:T(8,128)(2,1)}, u32[]{:S(2)}) copy-start(bf16[64,896]{1,0:T(8,128)(2,1)} %tok_ref.1) | copy-start | bytes 344068
  4.4 1.5 %copy-start.1 = (bf16[1,1024,896]{2,1,0:T(8,128)(2,1)S(1)}, bf16[1,1024,896]{2,1,0:T(8,128)(2,1)}, u32[]{:S(2)}) copy-start(bf16[1,1024,896]{2,1,0:T(8,128)(2,1)} %down_hbm.1) | copy-start | bytes 5505028

commit v2 on v1

v2 whole, which is shorter than its diff:
```python
import functools

import jax
import jax.numpy as jnp
import numpy as np
from jax import lax
from jax.experimental import pallas as pl
from jax.experimental.pallas import tpu as pltpu
from jax.sharding import PartitionSpec as P

MESH = pl.DeviceIdType.MESH
bf16 = jnp.bfloat16
f32 = jnp.float32

ROUTE_SCALE = 2.5
N = 8
TOK = 64
TOP = 8
QUARTER = 896
HID = 1024
LATENT = 512
KV = 576
PAGE = 16
GROUPS = ((0, 1, 7), (3, 5, 4), (2, 6))
STEPS = ((0, 1, 7, 2), (6, 3, 5, 4))
CHUNKS = (
    (0, STEPS[0], 128),
    (0, STEPS[1], 128),
    (1, STEPS[0], 128),
    (1, STEPS[1], 128),
    (2, STEPS[0], 80),
    (2, STEPS[1], 80),
)
LAST_LANES = 640
COUNT = len(CHUNKS)
MOST = max(chunk[2] for chunk in CHUNKS)


def dot(a, b):
    return jnp.dot(a, b, preferred_element_type=f32)


def put(ref, group, slots, rows):
    if group < 2:
        for i, at in enumerate(slots):
            ref[at] = rows[16 * i : 16 * i + 16].astype(bf16)
        return

    def folded(r):
        parts = [rows[r : r + 1, 128 * k : 128 * k + 128] for k in range(7)]
        return jnp.concatenate(parts + [jnp.zeros((1, 128), f32)], axis=0)

    many = len(slots)
    for i, at in enumerate(slots):
        head = rows[8 * i : 8 * i + 8]
        rest = jnp.concatenate([head[:, 512:QUARTER], folded(8 * many + i)], axis=1)
        ref[at, :, 0:512] = jnp.concatenate([head[:, 0:512], rest], axis=0).astype(bf16)
        ref[at, :, 512:640] = jnp.concatenate([folded(9 * many + i), jnp.zeros((8, 128), f32)], axis=0).astype(bf16)


def take(ref, group, slots):
    if group < 2:
        return jnp.concatenate([ref[at] for at in slots], axis=0)

    def unfolded(part):
        return jnp.concatenate([part[k : k + 1] for k in range(7)], axis=1)

    heads, first, second = [], [], []
    for at in slots:
        head = ref[at, :, 0:512].astype(f32)
        heads.append(jnp.concatenate([head[0:8], head[8:16, 0:384]], axis=1))
        first.append(unfolded(head[8:16, 384:512]))
        second.append(unfolded(ref[at, :, 512:640].astype(f32)))
    return jnp.concatenate(heads + first + second, axis=0).astype(bf16)


def kernel(
    tok_hbm,
    ids_hbm,
    scores_hbm,
    up_hbm,
    down_hbm,
    lat_hbm,
    gain_hbm,
    owner_ref,
    freq_hbm,
    out_ref,
    kv_ref,
    tok_ref,
    ids_ref,
    scores_ref,
    gain_ref,
    freq_ref,
    up_ref,
    down_ref,
    lat_ref,
    tok_0,
    tok_1,
    tok_2,
    line_meta,
    code_0,
    code_1,
    code_2,
    wsel_0,
    wsel_1,
    wsel_2,
    disp_out_0,
    disp_out_1,
    disp_in_0,
    disp_in_1,
    back_out_0,
    back_out_1,
    back_in_0,
    back_in_1,
    disp_out_2,
    disp_in_2,
    back_out_2,
    back_in_2,
    chain_out,
    chain_in,
    part_ref,
    full_out,
    full_in,
    hid_ref,
    pick_ref,
    sum_0,
    sum_1,
    sum_2,
    line_out,
    line_in,
    lat_out,
    lat_own,
    lat_in,
    load_sem,
    tok_send,
    tok_recv,
    meta_send,
    meta_recv,
    disp_send,
    disp_recv,
    back_send,
    back_recv,
    chain_send,
    chain_recv,
    full_send,
    full_recv,
    hid_send,
    hid_recv,
    line_send,
    line_recv,
    lat_send,
    lat_recv,
):
    group_tok = (tok_0, tok_1, tok_2)
    code = (code_0, code_1, code_2)
    wsel = (wsel_0, wsel_1, wsel_2)
    disp_out = (disp_out_0, disp_out_1, disp_out_2)
    disp_in = (disp_in_0, disp_in_1, disp_in_2)
    back_out = (back_out_0, back_out_1, back_out_2)
    back_in = (back_in_0, back_in_1, back_in_2)
    sums = (sum_0, sum_1, sum_2)
    ep = lax.axis_index("ep")
    x = lax.axis_index("dec")
    core = lax.rem(ep, 2)
    chip = lax.div(ep, 2)
    z = lax.div(chip, N)
    y = lax.rem(chip, N)
    on_z = core == 0
    mine = jnp.where(on_z, z, y)
    cross = jnp.where(on_z, y, z)

    def wrap(v):
        return lax.rem(v + 2 * N, N)

    def line_dev(step):
        place = wrap(mine + step)
        zz = jnp.where(on_z, place, z)
        yy = jnp.where(on_z, y, place)
        return ((zz * N + yy) * 2 + core, x)

    def expert_dev(step, c):
        place = wrap(cross + step)
        zz = jnp.where(on_z, z, place)
        yy = jnp.where(on_z, place, y)
        return ((zz * N + yy) * 2 + c, x)

    def source_dev(c_src, step):
        if c_src == 0:
            return ((z * N + wrap(y - step)) * 2, x)
        return ((wrap(z - step) * N + y) * 2 + 1, x)

    def dec_dev(step):
        return (ep, lax.rem(x + step + 4, 4))

    sent = []

    def send(src, dst, s_sem, r_sem, dev):
        copy = pltpu.make_async_remote_copy(
            src_ref=src, dst_ref=dst, send_sem=s_sem, recv_sem=r_sem, device_id=dev, device_id_type=MESH
        )
        copy.start()
        sent.append(copy)

    def arrived(dst, sem):
        pltpu.make_async_copy(dst, dst, sem).wait()

    loads = [
        pltpu.make_async_copy(src, dst, load_sem.at[i])
        for i, (src, dst) in enumerate(
            (
                (ids_hbm, ids_ref),
                (scores_hbm, scores_ref),
                (tok_hbm, tok_ref),
                (lat_hbm, lat_ref),
                (gain_hbm, gain_ref),
                (freq_hbm, freq_ref),
                (up_hbm.at[0], up_ref),
                (down_hbm.at[0], down_ref),
            )
        )
    ]
    for load in loads:
        load.start()

    barrier = pltpu.get_barrier_semaphore()

    def greet(dev):
        pl.semaphore_signal(barrier, inc=1, device_id=dev, device_id_type=MESH)

    greet(((z * N + y) * 2 + 1 - core, x))
    for step in range(1, N):
        for c in range(2):
            greet(((z * N + wrap(y + step)) * 2 + c, x))
            greet(((wrap(z + step) * N + y) * 2 + c, x))
    for step in range(1, 4):
        greet(dec_dev(step))

    loads[0].wait()
    loads[1].wait()
    gate = jax.nn.sigmoid(scores_ref[...])
    weight = ROUTE_SCALE * gate / jnp.sum(gate, axis=0, keepdims=True)
    line_meta[0] = jnp.concatenate([ids_ref[...].astype(f32), weight], axis=1)
    for group in range(2):
        group_tok[group][3] = jnp.zeros((TOK, QUARTER), bf16)
    loads[2].wait()

    pl.semaphore_wait(barrier, 4 * (N - 1) + 4)

    def place_of(rel):
        group = [rel in rels for rels in GROUPS].index(True)
        return group_tok[group].at[GROUPS[group].index(rel)]

    blocks = []

    def spread(src, rel, step, rows):
        at = len(blocks)
        dst = place_of(rel).at[pl.ds(*rows)]
        blocks.append((rel, rows, at))
        send(src.at[pl.ds(*rows)], dst, tok_send.at[at], tok_recv.at[at], line_dev(step))

    def taken(rel, rows):
        at = [b[2] for b in blocks if b[0] == rel and b[1] == rows][0]
        arrived(place_of(rel).at[pl.ds(*rows)], tok_recv.at[at])

    whole, low_half, high_half = (0, TOK), (0, TOK // 2), (TOK // 2, TOK // 2)
    for step in range(1, N):
        send(line_meta.at[0], line_meta.at[step], meta_send.at[step - 1], meta_recv.at[step - 1], line_dev(step))
    spread(tok_ref, 1, 1, whole)
    spread(tok_ref, 7, -1, whole)
    spread(tok_ref, 2, 2, low_half)
    spread(tok_ref, 6, -2, high_half)
    spread(tok_ref, 2, 2, high_half)
    spread(tok_ref, 6, -2, low_half)
    tok_0[0] = tok_ref[...]

    lane = lax.broadcasted_iota(jnp.int32, (TOK, TOK), 1)
    row = lax.broadcasted_iota(jnp.int32, (TOK, TOK), 0)
    owner_of = jnp.zeros((TOK, TOK), jnp.int32)
    page = jnp.int32(0)
    for p in range(4):
        owner_of = jnp.where((lane >> 4) == p, owner_ref[p], owner_of)
        page = page + jnp.where(owner_ref[p] == x, p, 0)
    wanted = lax.rem((row >> 4) + x, 4)
    order = jnp.where((owner_of == wanted) & ((lane & 15) == (row & 15)), 1.0, 0.0).astype(bf16)
    ordered = dot(order, tok_ref[...]).astype(bf16)
    loads[3].wait()
    latent = lax.dot_general(ordered, lat_ref[...], (((1,), (1,)), ((), ())), preferred_element_type=f32)
    lat_own[...] = latent[0:PAGE]
    lat_out[...] = latent[PAGE:].astype(bf16).reshape(3, PAGE, KV)
    for step in range(1, 4):
        send(lat_out.at[step - 1], lat_in.at[step - 1], lat_send.at[step - 1], lat_recv.at[step - 1], dec_dev(step))

    low = lax.broadcasted_iota(jnp.int32, (TOP, 128), 1) < TOK
    before_r = lax.broadcasted_iota(jnp.int32, (128, 128), 0)
    before_c = lax.broadcasted_iota(jnp.int32, (128, 128), 1)
    before = jnp.where((before_r < before_c) & ((before_r >> 6) == (before_c >> 6)), 1.0, 0.0).astype(bf16)
    number = lax.broadcasted_iota(jnp.int32, (16, 128), 0)
    place = lax.rem(cross + (number >> 1), N)
    expert = jnp.where(on_z, 16 * mine + 2 * place, 16 * place + 2 * mine) + (number & 1)
    expert = expert.astype(f32)

    coded = []

    def codes(group):
        if group in coded:
            return
        coded.append(group)
        rels = GROUPS[group]
        for rel in rels:
            if rel:
                arrived(line_meta.at[rel], meta_recv.at[rel - 1])
        for pair in range((len(rels) + 1) // 2):
            even = line_meta[rels[2 * pair]]
            if 2 * pair + 1 < len(rels):
                odd = line_meta[rels[2 * pair + 1]]
                ids = jnp.where(low, even, pltpu.roll(odd, TOK, 1))
            else:
                odd = jnp.zeros_like(even)
                ids = jnp.where(low, even, -1.0)
            weights = jnp.where(low, pltpu.roll(even, TOK, 1), odd)
            hits = jnp.zeros((16, 128), f32)
            chosen = jnp.zeros((16, 128), f32)
            for k in range(TOP):
                match = ids[k : k + 1, :] == expert
                hits = jnp.where(match, 1.0, hits)
                chosen = jnp.where(match, weights[k : k + 1, :], chosen)
            rank = dot(hits.astype(bf16), before)
            code[group][:, 128 * pair : 128 * pair + 128] = jnp.where(hits > 0.5, rank, -1.0)
            wsel[group][:, 128 * pair : 128 * pair + 128] = chosen

    wide_row = lax.broadcasted_iota(jnp.int32, (16, 256), 0)
    wide_block = lax.broadcasted_iota(jnp.int32, (16, 256), 1) >> 6
    wide_slot = (wide_row * 11) >> 5
    wide_pattern = jnp.where(wide_block == wide_row - 3 * wide_slot, wide_slot, -2).astype(f32)
    slim_row = lax.broadcasted_iota(jnp.int32, (8, 128), 0)
    slim_block = lax.broadcasted_iota(jnp.int32, (8, 128), 1) >> 6
    slim_pattern = jnp.where(slim_block == (slim_row & 1), slim_row >> 1, -2).astype(f32)

    def picks(group, steps, weighted):
        codes(group)

        def match(at, many, pat):
            value = wsel[group][at : at + many, :] if weighted else 1.0
            return jnp.where(code[group][at : at + many, :] == pat, value, 0.0)

        slots = [2 * step + c for step in steps for c in range(2)]
        if group < 2:
            return jnp.concatenate([match(at, 1, wide_pattern) for at in slots], axis=0)
        heads = [match(at, 1, slim_pattern) for at in slots]
        lasts = [
            match(2 * step, 2, jnp.where(slim_block[0:2] == block, 4.0, -2.0)) for block in range(2) for step in steps
        ]
        return jnp.concatenate(heads + lasts, axis=0)

    def stage_disp(j):
        group, steps, _ = CHUNKS[j]
        tok = group_tok[group]
        rows = dot(picks(group, steps, False).astype(bf16), tok[...].reshape(tok.shape[0] * TOK, QUARTER))
        put(disp_out[group], group, [2 * step + c for step in steps for c in range(2)], rows)
        out, into = disp_out[group], disp_in[group]
        for step in steps:
            slot = N * core + step
            s_at, r_at = 16 * group, 16 * group + slot
            if step == 0:
                pltpu.make_async_copy(out.at[core], into.at[slot], disp_recv.at[r_at]).start()
                other = 1 - core
                send(out.at[other], into.at[slot], disp_send.at[s_at + other], disp_recv.at[r_at], expert_dev(0, other))
            else:
                for c in range(2):
                    at = 2 * step + c
                    send(out.at[at], into.at[slot], disp_send.at[s_at + at], disp_recv.at[r_at], expert_dev(step, c))

    def stage_pick(j):
        group, steps, many = CHUNKS[j]
        tokens = group_tok[group].shape[0] * TOK
        pick_ref[j, 0:tokens, 0:many] = picks(group, steps, True).T.astype(bf16)

    def stage_latent():
        for step in range(1, 4):
            arrived(lat_in.at[step - 1], lat_recv.at[step - 1])
        loads[4].wait()
        loads[5].wait()
        total = lat_own[...]
        for step in range(3):
            total = total + lat_in[step].astype(f32)
        comp = total[:, 0:LATENT]
        scale = lax.rsqrt(jnp.sum(comp * comp, axis=1, keepdims=True) * (1.0 / LATENT) + 1e-6)
        kv_ref[:, 0:LATENT] = (comp * scale * gain_ref[...]).astype(bf16)
        half = (KV - LATENT) // 2
        first, second = total[:, LATENT : LATENT + half], total[:, LATENT + half :]
        token = (ep * TOK + page * PAGE + lax.broadcasted_iota(jnp.int32, (PAGE, half), 0)).astype(f32)
        angle = token * freq_ref[...]
        cos, sin = jnp.cos(angle), jnp.sin(angle)
        kv_ref[:, LATENT:] = jnp.concatenate(
            [first * cos - second * sin, second * cos + first * sin], axis=1
        ).astype(bf16)

    loaded = []

    def quarter_of(step):
        return pl.ds(pl.multiple_of(lax.rem(x + step + 4, 4) * 256, 256), 256)

    def stage_up(j):
        group, steps, many = CHUNKS[j]
        slots = [N * c + step for step in steps for c in range(2)]
        for slot in slots:
            arrived(disp_in[group].at[slot], disp_recv.at[16 * group + slot])
        block = take(disp_in[group], group, slots)
        if 6 not in loaded:
            loads[6].wait()
            loaded.append(6)
        part = dot(block, up_ref[:, quarter_of(2)])
        for d in range(2):
            chain_out[j, d, 0:many] = part[:, 128 * d : 128 * d + 128].astype(bf16)
            at = 2 * j + d
            send(
                chain_out.at[j, d, pl.ds(0, many)],
                chain_in.at[j, d, pl.ds(0, many)],
                chain_send.at[at],
                chain_recv.at[at],
                dec_dev(1 if d == 0 else -1),
            )
        part_ref[j, 0, 0:many] = dot(block, up_ref[:, quarter_of(1)])
        part_ref[j, 1, 0:many] = dot(block, up_ref[:, quarter_of(-1)])
        part_ref[j, 2, 0:many] = dot(block, up_ref[:, quarter_of(0)])

    def stage_chain(j):
        many = CHUNKS[j][2]
        for d in range(2):
            at = 2 * j + d
            arrived(chain_in.at[j, d, pl.ds(0, many)], chain_recv.at[at])
            for half in range(2):
                value = part_ref[j, d, 0:many, 128 * half : 128 * half + 128]
                if half == d:
                    value = value + chain_in[j, d, 0:many].astype(f32)
                full_out[j, d, half, 0:many] = value.astype(bf16)
            send(
                full_out.at[j, d, :, pl.ds(0, many)],
                full_in.at[j, d, :, pl.ds(0, many)],
                full_send.at[at],
                full_recv.at[at],
                dec_dev(1 if d == 0 else -1),
            )

    def stage_hidden(j):
        many = CHUNKS[j][2]
        for d in range(2):
            arrived(full_in.at[j, d, :, pl.ds(0, many)], full_recv.at[2 * j + d])
        for half in range(2):
            pre = part_ref[j, 2, 0:many, 128 * half : 128 * half + 128]
            pre = pre + full_in[j, 0, half, 0:many].astype(f32) + full_in[j, 1, half, 0:many].astype(f32)
            hid_ref[j, 0, half, 0:many] = (pre / (1.0 + jnp.exp(-pre))).astype(bf16)
        for d in range(2):
            send(
                hid_ref.at[j, 0, :, pl.ds(0, many)],
                hid_ref.at[j, 1 + d, :, pl.ds(0, many)],
                hid_send.at[4 * j + d],
                hid_recv.at[4 * j + d],
                dec_dev(1 if d == 0 else -1),
            )

    def stage_pass(j):
        many = CHUNKS[j][2]
        for d in range(2):
            arrived(hid_ref.at[j, 1 + d, :, pl.ds(0, many)], hid_recv.at[4 * j + d])
            send(
                hid_ref.at[j, 1 + d, d, pl.ds(0, many)],
                hid_ref.at[j, 3, d, pl.ds(0, many)],
                hid_send.at[4 * j + 2 + d],
                hid_recv.at[4 * j + 2 + d],
                dec_dev(1 if d == 0 else -1),
            )

    def stage_down(j):
        group, steps, many = CHUNKS[j]
        if 7 not in loaded:
            loads[7].wait()
            loaded.append(7)
        total = None
        for place, step in ((0, 0), (1, -1), (2, 1), (3, 2)):
            if place == 3:
                for d in range(2):
                    arrived(hid_ref.at[j, 3, d, pl.ds(0, many)], hid_recv.at[4 * j + 2 + d])
            hidden = jnp.concatenate([hid_ref[j, place, 0, 0:many], hid_ref[j, place, 1, 0:many]], axis=1)
            term = dot(hidden, down_ref[quarter_of(step), :])
            total = term if total is None else total + term
        put(back_out[group], group, [N * c + step for step in steps for c in range(2)], total)
        out, into = back_out[group], back_in[group]
        for step in steps:
            slot = 2 * step + core
            s_at, r_at = 16 * group, 16 * group + slot
            if step == 0:
                own, other = N * core, N * (1 - core)
                pltpu.make_async_copy(out.at[own], into.at[slot], back_recv.at[r_at]).start()
                mate = ((z * N + y) * 2 + 1 - core, x)
                send(out.at[other], into.at[slot], back_send.at[s_at + other], back_recv.at[r_at], mate)
            else:
                for c in range(2):
                    at = N * c + step
                    send(out.at[at], into.at[slot], back_send.at[s_at + at], back_recv.at[r_at], source_dev(c, step))

    summed = [0, 0, 0]

    def stage_sum(j):
        group, steps, many = CHUNKS[j]
        slots = [2 * step + c for step in steps for c in range(2)]
        for slot in slots:
            arrived(back_in[group].at[slot], back_recv.at[16 * group + slot])
        block = take(back_in[group], group, slots)
        rels = GROUPS[group]
        total = dot(pick_ref[j, 0 : TOK * len(rels), 0:many], block)
        if summed[group]:
            total = total + sums[group][...]
        summed[group] += 1
        if summed[group] < len([c for c in CHUNKS if c[0] == group]):
            sums[group][...] = total
            return
        if group == 0:
            sums[0][0:TOK] = total[0:TOK]
        def give(rel, step, rows):
            at = rel - 1 if rel != 4 or rows == low_half else 7
            part = pl.ds(*rows)
            send(line_out.at[rel - 1, part], line_in.at[rel - 1, part], line_send.at[at], line_recv.at[at], line_dev(step))

        if group == 2:
            for rel, part in ((3, whole), (5, whole), (4, low_half), (4, high_half)):
                at = rel - 1 if rel != 4 or part == low_half else 7
                arrived(line_in.at[rel - 1, pl.ds(*part)], line_recv.at[at])
            middle = line_in[3].astype(f32)
            total = total + jnp.concatenate(
                [
                    line_in[2, 0:32].astype(f32) + middle[0:32],
                    line_in[2, 32:64].astype(f32),
                    line_in[4, 0:32].astype(f32),
                    line_in[4, 32:64].astype(f32) + middle[32:64],
                ],
                axis=0,
            )
        for i, rel in enumerate(rels):
            if rel:
                line_out[rel - 1] = total[TOK * i : TOK * i + TOK].astype(bf16)
        if group == 0:
            give(1, -1, whole)
            give(7, 1, whole)
        elif group == 1:
            give(4, -2, low_half)
            give(4, 2, high_half)
            give(3, -1, whole)
            give(5, 1, whole)
        else:
            give(2, -2, whole)
            give(6, 2, whole)

    def wait_near():
        for rel in GROUPS[0][1:]:
            taken(rel, whole)

    def pass_far():
        taken(2, low_half)
        spread(place_of(2), 4, 2, low_half)
        taken(6, high_half)
        spread(place_of(6), 4, -2, high_half)
        taken(2, high_half)
        spread(place_of(2), 3, 1, whole)
        taken(6, low_half)
        spread(place_of(6), 5, -1, whole)

    def wait_far():
        for rel, rows in ((3, whole), (5, whole), (4, low_half), (4, high_half)):
            taken(rel, rows)

    wait_near()
    stage_disp(0)
    pass_far()
    stage_pick(5)
    stage_disp(5)
    stage_pick(0)
    stage_up(0)
    stage_disp(4)
    stage_chain(0)
    wait_far()
    stage_disp(3)
    stage_latent()
    stage_disp(2)
    stage_up(5)
    stage_up(4)
    stage_hidden(0)
    stage_disp(1)
    stage_chain(5)
    stage_chain(4)
    stage_up(3)
    stage_pass(0)
    stage_hidden(5)
    stage_hidden(4)
    stage_chain(3)
    stage_pass(5)
    stage_up(2)
    stage_pass(4)
    stage_up(1)
    stage_pick(2)
    stage_hidden(3)
    stage_down(5)
    stage_chain(2)
    stage_chain(1)
    stage_pick(1)
    stage_down(4)
    stage_pick(3)
    stage_pass(3)
    stage_down(0)
    stage_hidden(2)
    stage_pick(4)
    stage_hidden(1)
    stage_pass(2)
    stage_down(3)
    stage_pass(1)
    stage_down(2)
    stage_down(1)
    stage_sum(2)
    stage_sum(3)
    stage_sum(0)
    stage_sum(1)
    stage_sum(4)
    stage_sum(5)

    total = sum_0[0:TOK]
    for rel in (1, 7, 2, 6):
        arrived(line_in.at[rel - 1], line_recv.at[rel - 1])
        total = total + line_in[rel - 1].astype(f32)
    out_ref[...] = total.astype(bf16)

    for copy in sent:
        copy.wait_send()


def on_device(tokens, expert_ids, route_scores, up_weight, down_weight, latent_weight, latent_norm_gain, page_owner):
    half = (KV - LATENT) // 2
    freq = np.power(10000.0, -np.arange(half, dtype=np.float64) / half).astype(np.float32)
    vmem = pl.BlockSpec(memory_space=pltpu.VMEM)
    hbm = pl.BlockSpec(memory_space=pl.ANY)
    smem = pl.BlockSpec(memory_space=pltpu.SMEM)
    dma = pltpu.SemaphoreType.DMA
    return pl.pallas_call(
        kernel,
        out_shape=(
            jax.ShapeDtypeStruct((TOK, QUARTER), bf16),
            jax.ShapeDtypeStruct((PAGE, KV), bf16),
        ),
        in_specs=[hbm, hbm, hbm, hbm, hbm, hbm, hbm, smem, hbm],
        out_specs=(vmem, vmem),
        scratch_shapes=[
            pltpu.VMEM((TOK, QUARTER), bf16),
            pltpu.VMEM((TOP, TOK), jnp.int32),
            pltpu.VMEM((TOP, TOK), f32),
            pltpu.VMEM((1, LATENT), f32),
            pltpu.VMEM((1, half), f32),
            pltpu.VMEM((QUARTER, HID), bf16),
            pltpu.VMEM((HID, QUARTER), bf16),
            pltpu.VMEM((KV, QUARTER), bf16),
            pltpu.VMEM((4, TOK, QUARTER), bf16),
            pltpu.VMEM((4, TOK, QUARTER), bf16),
            pltpu.VMEM((2, TOK, QUARTER), bf16),
            pltpu.VMEM((N, TOP, 128), f32),
        ]
        + [pltpu.VMEM((16, lanes), f32) for lanes in (256, 256, 128)] * 2
        + [pltpu.VMEM((16, 16, QUARTER), bf16)] * 8
        + [pltpu.VMEM((16, 16, LAST_LANES), bf16)] * 4
        + [
            pltpu.VMEM((COUNT, 2, MOST, 128), bf16),
            pltpu.VMEM((COUNT, 2, MOST, 128), bf16),
            pltpu.VMEM((COUNT, 3, MOST, 256), f32),
            pltpu.VMEM((COUNT, 2, 2, MOST, 128), bf16),
            pltpu.VMEM((COUNT, 2, 2, MOST, 128), bf16),
            pltpu.VMEM((COUNT, 4, 2, MOST, 128), bf16),
            pltpu.VMEM((COUNT, 256, MOST), bf16),
            pltpu.VMEM((3 * TOK, QUARTER), f32),
            pltpu.VMEM((3 * TOK, QUARTER), f32),
            pltpu.VMEM((2 * TOK, QUARTER), f32),
            pltpu.VMEM((7, TOK, QUARTER), bf16),
            pltpu.VMEM((7, TOK, QUARTER), bf16),
            pltpu.VMEM((3, PAGE, KV), bf16),
            pltpu.VMEM((PAGE, KV), f32),
            pltpu.VMEM((3, PAGE, KV), bf16),
        ]
        + [
            dma((count,))
            for count in (8, 10, 10, 7, 7, 48, 48, 48, 48)
            + (2 * COUNT,) * 4
            + (4 * COUNT, 4 * COUNT, 8, 8, 3, 3)
        ],
        compiler_params=pltpu.CompilerParams(
            collective_id=0, has_side_effects=True, vmem_limit_bytes=60 * 1024 * 1024
        ),
    )(
        tokens,
        expert_ids.T,
        route_scores.T,
        up_weight,
        down_weight,
        latent_weight.T,
        latent_norm_gain.reshape(1, LATENT),
        page_owner,
        jnp.asarray(freq).reshape(1, half),
    )


def solution(mesh):
    placed = (
        P("ep", "dec"),
        P("ep", None),
        P("ep", None),
        P("ep", "dec", None),
        P("ep", None, "dec"),
        P("dec", None),
        P(),
        P("ep"),
    )
    return jax.shard_map(
        on_device,
        mesh=mesh,
        in_specs=placed,
        out_specs=(P("ep", "dec"), P(("ep", "dec"), None)),
        check_vma=False,
    )
```

time: 102 us -> 84.5 us (0.83)
  the two profiles are of different devices: /device:TPU:22 before, /device:TPU:16 now
where the time goes in v2:
time: 84.5 us; the launch traced here: 84.3 us
  Pallas kernels  80.8 us (96%)
  local copies, waits for them, and re-layouts  2.89 us (3%)
    pallas_call x1, Pallas kernels, on_device(): pl.pallas_call(kernel, out_shape=(jax.ShapeDtypeStruct((TOK, QUARTER), bf...  80.8 us
    unnamed x2, local copies, waits for them, and re-layouts  2.89 us

profile of v2, /device:TPU:16, one launch (start us, length us, event | category | flops | bytes accessed | tf_op | source)
XLA Modules:
  0.0 84.3 jit_solution(8118615483015215380)
XLA Ops:
  0.6 80.8 %shard_map.104 = (bf16[64,896]{1,0:T(8,128)(2,1)}, bf16[16,576]{1,0:T(8,128)(2,1)}) custom-call(bf16[64,896]{1,0:T(8,128)(2,1)} %tok_hbm.1, s32[8,64]{1,0:T(8,128)} %bitcast.5, f32[8,64]{1,0:T(8,128)} %bitcast.6, bf16[1,896,1024]{2,1,0:T(8,128)(2,1)} %up_hbm.1, bf16[1,1024,896]{2,1,0:T(8,128)(2,1)} %down_hbm.1, bf16[576,896]{1,0:T(8,128)(2,1)} %bitcast.4, ...), custom_call_target="tpu_custom_call" | custom-call | tf_op jit(solution)/shard_map/pallas_call | solution.py:642
  81.4 1.6 %copy.13 = bf16[64,896]{1,0:T(8,128)(2,1)} copy(bf16[64,896]{1,0:T(8,128)(2,1)} %get-tuple-element.4) | data formatting | bytes 229376
  83.0 1.3 %copy.14 = bf16[16,576]{1,0:T(8,128)(2,1)} copy(bf16[16,576]{1,0:T(8,128)(2,1)} %get-tuple-element.5) | data formatting | bytes 36864

commit v3 on v2

--- a/solution.py
+++ b/solution.py
@@ -204,6 +204,19 @@
     def arrived(dst, sem):
         pltpu.make_async_copy(dst, dst, sem).wait()
 
+    barrier = pltpu.get_barrier_semaphore()
+
+    def greet(dev):
+        pl.semaphore_signal(barrier, inc=1, device_id=dev, device_id_type=MESH)
+
+    greet(((z * N + y) * 2 + 1 - core, x))
+    for step in range(1, N):
+        for c in range(2):
+            greet(((z * N + wrap(y + step)) * 2 + c, x))
+            greet(((wrap(z + step) * N + y) * 2 + c, x))
+    for step in range(1, 4):
+        greet(dec_dev(step))
+
     loads = [
         pltpu.make_async_copy(src, dst, load_sem.at[i])
         for i, (src, dst) in enumerate(
@@ -221,19 +234,6 @@
     ]
     for load in loads:
         load.start()
-
-    barrier = pltpu.get_barrier_semaphore()
-
-    def greet(dev):
-        pl.semaphore_signal(barrier, inc=1, device_id=dev, device_id_type=MESH)
-
-    greet(((z * N + y) * 2 + 1 - core, x))
-    for step in range(1, N):
-        for c in range(2):
-            greet(((z * N + wrap(y + step)) * 2 + c, x))
-            greet(((wrap(z + step) * N + y) * 2 + c, x))
-    for step in range(1, 4):
-        greet(dec_dev(step))
 
     loads[0].wait()
     loads[1].wait()
@@ -578,9 +578,9 @@
     stage_up(0)
     stage_disp(4)
     stage_chain(0)
+    stage_latent()
     wait_far()
     stage_disp(3)
-    stage_latent()
     stage_disp(2)
     stage_up(5)
     stage_up(4)
@@ -610,8 +610,8 @@
     stage_hidden(2)
     stage_pick(4)
     stage_hidden(1)
+    stage_down(3)
     stage_pass(2)
-    stage_down(3)
     stage_pass(1)
     stage_down(2)
     stage_down(1)
@@ -622,13 +622,15 @@
     stage_sum(4)
     stage_sum(5)
 
+    for copy in sent[:-8]:
+        copy.wait_send()
     total = sum_0[0:TOK]
     for rel in (1, 7, 2, 6):
         arrived(line_in.at[rel - 1], line_recv.at[rel - 1])
         total = total + line_in[rel - 1].astype(f32)
     out_ref[...] = total.astype(bf16)
 
-    for copy in sent:
+    for copy in sent[-8:]:
         copy.wait_send()
 
 

time: 84.5 us -> 82.6 us (0.978)
  Pallas kernels: 80.8 us -> 78.9 us
    pallas_call x1, Pallas kernels: 80.8 us -> 78.9 us  [on_device(): pl.pallas_call(kernel, out_shape=(jax.ShapeDtypeStruct((TOK, QUARTER), bf...]
where the time goes in v3:
time: 82.6 us; the launch traced here: 82.4 us
  Pallas kernels  78.9 us (96%)
  local copies, waits for them, and re-layouts  2.89 us (3%)
    pallas_call x1, Pallas kernels, on_device(): pl.pallas_call(kernel, out_shape=(jax.ShapeDtypeStruct((TOK, QUARTER), bf...  78.9 us
    unnamed x2, local copies, waits for them, and re-layouts  2.89 us

profile of v3, /device:TPU:16, one launch (start us, length us, event | category | flops | bytes accessed | tf_op | source)
XLA Modules:
  0.0 82.4 jit_solution(17448035519731560208)
XLA Ops:
  0.6 78.9 %shard_map.104 = (bf16[64,896]{1,0:T(8,128)(2,1)}, bf16[16,576]{1,0:T(8,128)(2,1)}) custom-call(bf16[64,896]{1,0:T(8,128)(2,1)} %tok_hbm.1, s32[8,64]{1,0:T(8,128)} %bitcast.5, f32[8,64]{1,0:T(8,128)} %bitcast.6, bf16[1,896,1024]{2,1,0:T(8,128)(2,1)} %up_hbm.1, bf16[1,1024,896]{2,1,0:T(8,128)(2,1)} %down_hbm.1, bf16[576,896]{1,0:T(8,128)(2,1)} %bitcast.4, ...), custom_call_target="tpu_custom_call" | custom-call | tf_op jit(solution)/shard_map/pallas_call | solution.py:644
  79.5 1.6 %copy.13 = bf16[64,896]{1,0:T(8,128)(2,1)} copy(bf16[64,896]{1,0:T(8,128)(2,1)} %get-tuple-element.4) | data formatting | bytes 229376
  81.1 1.3 %copy.14 = bf16[16,576]{1,0:T(8,128)(2,1)} copy(bf16[16,576]{1,0:T(8,128)(2,1)} %get-tuple-element.5) | data formatting | bytes 36864
